TPU v7x, 32 devices: a whole 2x2x4 slice. The times are simulated.
32 devices in a mesh: clip: 2 (over y), row: 4 (over z), col: 2 (over x), pol: 2 (over core).
Axes of the slice: x: 2, y: 2, z: 4, core: 2. Of those that a mesh axis runs over, the one named last changes fastest.
Arguments:
- tcc_blocks: bfloat16 [8, 2, 2, 16, 2, 256, 256], P(('clip', 'row'), 'col', 'pol'), parts along dimension 0, may hold values from -32 to 32
- slot_rows: int32 [8, 2, 2, 16], P(('clip', 'row'), 'col', 'pol'), parts along dimension 0, may hold values from 0 to 3, as said below
- slot_cols: int32 [8, 2, 2, 16], P(('clip', 'row'), 'col', 'pol'), parts along dimension 0, may hold values from 0 to 3
- slot_count: int32 [8, 2, 2], P(('clip', 'row'), 'col', 'pol'), parts along dimension 0, may hold values from 1 to 16, as said below
- subspace: bfloat16 [8192, 256], P(('clip', 'row', 'col', 'pol')), parts along dimension 0, may hold values from -6 to 6
Outputs:
- subspace_out: float32 [8192, 256], P(('clip', 'row', 'col', 'pol')), parts along dimension 0
- gram_factor: float32 [256, 128], P('clip'), parts along dimension 0
There are 2 independent parts, one for each index of `clip`. A program takes and returns all parts, laid end to end along the dimension named above; each array names one. Nothing has to cross between parts.
Inputs may be any that keep to these rules, and one draw needn't show every extreme that they name: Within one device position the pairs of slot_rows and slot_cols of all 16 slots are distinct. `slot_count`: some device position has all 16 slots live.
All inputs are finite; a program needn't handle non-finite values.
Results may differ from a plain program's by a relative error of at most 0.003.
Values may be sent and summed in bfloat16 or wider, within the bound.
A program may use at most 64 MiB of HBM per device.

v0:
```python
import jax
import jax.numpy as jnp
from jax import lax
from jax.sharding import PartitionSpec as P

ITERS = 2


def combine_parts(product, block_size, half_width):
    real_part = product[:block_size, :half_width] - product[block_size:, half_width:]
    imag_part = product[:block_size, half_width:] + product[block_size:, :half_width]
    return jnp.concatenate([real_part, imag_part], axis=1)


def accumulate(running, blocks, row_ids, fetch_rows, first, last):
    block_size = blocks.shape[2]
    half_width = running.shape[2] // 2

    def visit_slot(position, partial_value):
        block_data = lax.dynamic_index_in_dim(blocks, position, 0, keepdims=False)
        product = jnp.dot(block_data, fetch_rows(position), preferred_element_type=jnp.float32)
        target = row_ids[position]
        before = lax.dynamic_index_in_dim(partial_value, target, 0, keepdims=False)
        return lax.dynamic_update_index_in_dim(
            partial_value, before + combine_parts(product, block_size, half_width), target, 0
        )

    return lax.fori_loop(jnp.int32(first), jnp.int32(last), visit_slot, running)


def on_device(tcc_blocks, slot_rows, slot_cols, slot_count, subspace):
    block_size = subspace.shape[0]
    full_width = subspace.shape[1]
    half_width = full_width // 2
    row_group = lax.axis_size("row")
    col_group = lax.axis_size("col") * lax.axis_size("pol")
    slot_total = tcc_blocks.shape[3]
    blocks = tcc_blocks.reshape(slot_total, 2 * block_size, block_size)
    row_ids = slot_rows.reshape(slot_total)
    col_ids = slot_cols.reshape(slot_total)
    live_count = slot_count.reshape(())
    order_total = block_size * row_group * col_group
    current = subspace
    for iteration in range(ITERS):
        panel_rows = lax.all_gather(current, "row", axis=0, tiled=True).reshape(
            row_group, block_size, full_width
        )

        def fetch_local(position):
            return lax.dynamic_index_in_dim(panel_rows, col_ids[position], 0, keepdims=False)

        partial_value = jnp.zeros((col_group, block_size, full_width), jnp.float32)
        partial_value = accumulate(partial_value, blocks, row_ids, fetch_local, 0, live_count)
        own_rows = lax.psum_scatter(
            partial_value.reshape(col_group * block_size, full_width),
            ("col", "pol"),
            scatter_dimension=0,
            tiled=True,
        )
        halves = own_rows.reshape(block_size, 2, half_width)
        local_gram = jnp.einsum("nak,nal->kl", halves, halves, precision=lax.Precision.HIGHEST)
        gram_sum = lax.psum(local_gram, ("row", "col", "pol")) / (2.0 * order_total)
        factor = jnp.linalg.cholesky(gram_sum)
        solved = lax.linalg.triangular_solve(
            factor,
            own_rows.reshape(2 * block_size, half_width),
            left_side=False,
            lower=True,
            transpose_a=True,
        )
        orthonormal = solved.reshape(block_size, full_width)
        current = orthonormal.astype(jnp.bfloat16)
    return (orthonormal, factor)


def solution(mesh):
    placed = (
        P(("clip", "row"), "col", "pol", None, None, None, None),
        P(("clip", "row"), "col", "pol", None),
        P(("clip", "row"), "col", "pol", None),
        P(("clip", "row"), "col", "pol"),
        P(("clip", "row", "col", "pol"), None),
    )
    return jax.shard_map(
        on_device,
        mesh=mesh,
        in_specs=placed,
        out_specs=(P(("clip", "row", "col", "pol"), None), P("clip", None)),
        check_vma=False,
    )
```

profile of v0, /device:TPU:0, one launch (start us, length us, event | category | flops | bytes accessed | tf_op | source)
XLA Modules:
  0.0 589.5 jit_solution(14261678323394172090)
XLA Ops:
  7.2 17.6 %all_gather.6 = bf16[1024,256]{1,0:T(8,128)(2,1)S(1)} all-gather(bf16[256,256]{1,0:T(8,128)(2,1)} %param.16), channel_id=1, replica_groups=mesh['clip'=2,'row'=4,'col'=2,'pol'=2] {'row'}, dimensions={0}, use_global_device_ids=true | all-gather | bytes 655360 | tf_op jit(solution)/shard_map/all_gather | solution.py:45
  24.9 52.8 %while.20 = (s32[]{:T(128)}, f32[4,256,256]{2,1,0:T(8,128)S(1)}, s32[]{:T(128)}, s32[16]{0:T(128)}, bf16[16,512,256]{2,1,0:T(8,128)(2,1)}, /*index=5*/s32[16]{0:...) while((s32[]{:T(128)}, f32[4,256,256]{2,1,0:T(8,128)S(1)}, ...), condition=%wide.region_1.2_spmd, body=%wide.region_0.1_spmd.sunk | while | flops 67305480 | bytes 4587771 | solution.py:28
  25.5 1.2 dynamic_slice.65
  28.7 1.2 fusion.44
  30.0 1.2 dynamic_slice.64
  34.2 1.2 dynamic_slice.65
  37.4 1.2 fusion.44
  38.7 1.2 dynamic_slice.64
  42.9 1.2 dynamic_slice.65
  46.1 1.2 fusion.44
  47.4 1.2 dynamic_slice.64
  51.6 1.2 dynamic_slice.65
  54.8 1.2 fusion.44
  56.1 1.2 dynamic_slice.64
  60.3 1.2 dynamic_slice.65
  63.5 1.2 fusion.44
  64.7 1.2 dynamic_slice.64
  69.0 1.2 dynamic_slice.65
  72.2 1.2 fusion.44
  73.4 1.2 dynamic_slice.64
  77.7 1.0 copy-done.1
  78.7 112.7 %reduce-scatter.3.cloned.1.call-done = f32[256,256]{1,0:T(8,128)} async-done(((f32[1024,256]{1,0:T(8,128)}), f32[256,256]{1,0:T(8,128)}) %reduce-scatter.3.cloned.1.call-update) | async-done | bytes 262160 | tf_op jit(solution)/shard_map/reduce_scatter | solution.py:54
  191.4 2.2 convolution_bitcast_fusion.3
  193.8 1.0 reshape.67
  194.7 85.6 %all-reduce.3.cloned.1.call-done = f32[128,128]{0,1:T(8,128)} async-done(((f32[128,128]{0,1:T(8,128)}), f32[128,128]{0,1:T(8,128)}) %all-reduce.3.cloned.1.call-update) | async-done | bytes 65552 | tf_op jit(solution)/shard_map/psum | solution.py:62
  280.4 0.8 broadcast_multiply_fusion.1
  281.3 0.9 fusion.25
  282.2 11.7 %cholesky.44 = f32[128,128]{1,0:T(8,128)S(1)} custom-call(f32[128,128]{1,0:T(8,128)S(1)} %fusion.25), custom_call_target="Cholesky" | custom-call | tf_op jit(solution)/shard_map/jit(cholesky)/cholesky | solution.py:63
  293.9 0.6 compare_reduce_fusion.1
  294.6 0.7 fusion.21
  295.2 9.8 %custom-call.6 = f32[1,128,128]{1,2,0:T(8,128)S(1)} custom-call(f32[1,128,128]{2,1,0:T(8,128)S(1)} %fusion.21), custom_call_target="InvertDiagBlocksLowerTriangular" | custom-call | tf_op jit(solution)/shard_map/triangular_solve/custom-call.0 | solution.py:64
  305.6 17.4 %all_gather.7 = bf16[1024,256]{1,0:T(8,128)(2,1)S(1)} all-gather(bf16[256,256]{1,0:T(8,128)(2,1)S(1)} %convert_element_type.7), channel_id=1, replica_groups=mesh['clip'=2,'row'=4,'col'=2,'pol'=2] {'row'}, dimensions={0}, use_global_device_ids=true | all-gather | bytes 655360 | tf_op jit(solution)/shard_map/all_gather | solution.py:45
  323.1 44.9 %while.21 = (s32[]{:T(128)}, f32[4,256,256]{2,1,0:T(8,128)S(1)}, s32[]{:T(128)}, s32[16]{0:T(128)S(1)}, bf16[16,512,256]{2,1,0:T(8,128)(2,1)}, /*index=5*/s32[16...) while((s32[]{:T(128)}, f32[4,256,256]{2,1,0:T(8,128)S(1)}, ...), condition=%wide.region_7.10_spmd, body=%wide.region_6.9_spmd.sunk | while | flops 67305480 | bytes 4587771 | solution.py:28
  323.8 0.6 dynamic_slice.70
  326.3 1.2 fusion.48
  327.6 0.6 dynamic_slice.69
  331.2 0.6 dynamic_slice.70
  333.7 1.2 fusion.48
  335.0 0.6 dynamic_slice.69
  338.6 0.6 dynamic_slice.70
  341.1 1.2 fusion.48
  342.4 0.6 dynamic_slice.69
  345.9 0.6 dynamic_slice.70
  348.5 1.2 fusion.48
  349.7 0.6 dynamic_slice.69
  353.3 0.6 dynamic_slice.70
  355.8 1.2 fusion.48
  357.1 0.6 dynamic_slice.69
  360.7 0.6 dynamic_slice.70
  363.2 1.2 fusion.48
  364.5 0.6 dynamic_slice.69
  368.1 1.0 copy-done
  369.3 98.3 %reduce-scatter.5.cloned.1.call-done = f32[256,256]{1,0:T(8,128)} async-done(((f32[1024,256]{1,0:T(8,128)}), f32[256,256]{1,0:T(8,128)}) %reduce-scatter.5.cloned.1.call-update) | async-done | bytes 262160 | tf_op jit(solution)/shard_map/reduce_scatter | solution.py:54
  467.6 2.2 convolution_bitcast_fusion.2
  469.9 1.0 reshape.71
  470.8 85.5 %all-reduce.5.cloned.1.call-done = f32[128,128]{0,1:T(8,128)} async-done(((f32[128,128]{0,1:T(8,128)}), f32[128,128]{0,1:T(8,128)}) %all-reduce.5.cloned.1.call-update) | async-done | bytes 65552 | tf_op jit(solution)/shard_map/psum | solution.py:62
  556.3 0.8 broadcast_multiply_fusion
  557.2 0.9 fusion.23
  558.1 11.7 %cholesky.55 = f32[128,128]{1,0:T(8,128)S(1)} custom-call(f32[128,128]{1,0:T(8,128)S(1)} %fusion.23), custom_call_target="Cholesky" | custom-call | tf_op jit(solution)/shard_map/jit(cholesky)/cholesky | solution.py:63
  569.8 0.6 compare_reduce_fusion
  570.5 1.3 select_bitcast_fusion
  571.8 9.8 %custom-call.7 = f32[1,128,128]{1,2,0:T(8,128)S(1)} custom-call(f32[1,128,128]{2,1,0:T(8,128)S(1)} %get-tuple-element.110), custom_call_target="InvertDiagBlocksLowerTriangular" | custom-call | tf_op jit(solution)/shard_map/triangular_solve/custom-call.0 | solution.py:64
  581.6 0.4 convolution_bitcast_fusion
  582.1 0.8 reshape.72
  (96 shorter events, 6.0 us)
Async XLA Ops:
  7.2 184.3 %reduce-scatter.3.cloned.1.call-start = ((), (), s32[]{:S(2)}) async-start(), calls=%async_computation.2 | async-start | bytes 1310720 | tf_op jit(solution)/shard_map/reduce_scatter | solution.py:54
  77.7 1.0 copy-start.1
  77.7 245.4 %copy-start.2 = (s32[16]{0:T(128)S(1)}, s32[16]{0:T(128)}, u32[]{:S(2)}) copy-start(s32[16]{0:T(128)} %get-tuple-element.295) | copy-start | bytes 196
  77.7 245.4 %copy-start.3 = (s32[16]{0:T(128)S(1)}, s32[16]{0:T(128)}, u32[]{:S(2)}) copy-start(s32[16]{0:T(128)} %get-tuple-element.296) | copy-start | bytes 196
  78.7 201.7 %all-reduce.3.cloned.1.call-start = ((), (), s32[]{:S(2)}) async-start(), calls=%async_computation.3 | async-start | bytes 131072 | tf_op jit(solution)/shard_map/psum | solution.py:62
  193.7 273.9 %reduce-scatter.5.cloned.1.call-start = ((), (), s32[]{:S(2)}) async-start(), calls=%async_computation.4 | async-start | bytes 1310720 | tf_op jit(solution)/shard_map/reduce_scatter | solution.py:54
  368.1 1.0 copy-start
  369.1 187.2 %all-reduce.5.cloned.1.call-start = ((), (), s32[]{:S(2)}) async-start(), calls=%async_computation.5 | async-start | bytes 131072 | tf_op jit(solution)/shard_map/psum | solution.py:62
Sparse Core Ops, SparseCore 0:
  78.8 112.6 reduce-scatter.2
  195.9 84.4 all-reduce.2
  369.2 98.3 reduce-scatter.4
  471.9 84.3 all-reduce.4
where the time goes:
time: 594 us; the launch traced here: 589 us
  waiting for transfers between devices  382 us (64%)
  loops' own time  56.6 us (10%)
  other arithmetic  50.6 us (9%)
  blocking collectives  35 us (6%)
  local copies, waits for them, and re-layouts  30.9 us (5%)
  matrix products  20 us (3%)
  between operations  13.9 us (2%)
    reduce_scatter x2, waiting for transfers between devices, on_device(): lax.psum_scatter(partial_value.reshape(col_group * block_size, full_width...  211 us
    psum x2, waiting for transfers between devices, on_device(): gram_sum = lax.psum(local_gram, ('row', 'col', 'pol')) / (2.0 * order_total)  171 us
    another operation x2, loops' own time, accumulate(): return lax.fori_loop(jnp.int32(first), jnp.int32(last), visit_slot, running)  56.6 us
    all_gather x2, blocking collectives, on_device(): lax.all_gather(current, 'row', axis=0, tiled=True)  35 us
    another operation x6, other arithmetic, on_device(): factor = jnp.linalg.cholesky(gram_sum)  24.8 us
    another operation x4, other arithmetic, on_device(): lax.linalg.triangular_solve(factor, own_rows.reshape(2 * block_size, half...  21.6 us
    dot_general x12, matrix products, visit_slot(): jnp.dot(block_data, fetch_rows(position), preferred_element_type=jnp.floa...  14.7 us
  transfers between devices with their start and end apart: 4, of which 4 were waited for; matrix products, arithmetic and copies ran while one was open for 0% of the time, Pallas kernels for 0%

commit v1 on v0

v1 whole, which is shorter than its diff:
```python
import functools

import jax
import jax.numpy as jnp
from jax import lax
from jax.experimental import pallas as pl
from jax.experimental.pallas import tpu as pltpu
from jax.sharding import PartitionSpec as P

ITERS = 2
F32 = jnp.float32
BF16 = jnp.bfloat16
HI = lax.Precision.HIGHEST
PANEL = 8


def factor_and_inverse(gram):
    order = gram.shape[0]
    lane = lax.broadcasted_iota(jnp.int32, (1, order), 1)
    lanes = lax.broadcasted_iota(jnp.int32, (PANEL, order), 1)
    subs = lax.broadcasted_iota(jnp.int32, (PANEL, order), 0)
    upper_rows, inverse_rows = [], []
    rest = gram
    for start in range(0, order, PANEL):
        top, rest = rest[:PANEL], rest[PANEL:]
        left = order - start - PANEL
        diag = [jnp.broadcast_to(top[:, start + k:start + k + 1], (PANEL, order)) for k in range(PANEL)]
        if left:
            below = [jnp.broadcast_to(rest[:, start + k:start + k + 1], (left, order)) for k in range(PANEL)]
            rest = jnp.where((lane >= start) & (lane < start + PANEL), 0.0, rest)
        pivots = diag[0]
        for k in range(PANEL):
            here = start + k
            inv = 1.0 / diag[k][k:k + 1]
            under = jnp.where(subs > k, diag[k], 0.0)
            mults = {l: diag[l][k:k + 1] * inv for l in range(k + 1, PANEL)}
            row = jnp.where(lane == here, 1.0, top[k:k + 1]) * inv
            if k:
                pivots = jnp.where(subs == k, diag[k], pivots)
            top = jnp.where((lanes == here) & (subs > k), 0.0, top) - under * row
            for l in range(k + 1, PANEL):
                diag[l] = diag[l] - under * mults[l]
            if left:
                row = jnp.where((lane > here) & (lane < start + PANEL), 0.0, row)
                rest = rest - below[k] * row
                for l in range(k + 1, PANEL):
                    below[l] = below[l] - below[k] * mults[l]
        root = lax.rsqrt(pivots)
        scaled = top * root
        upper_rows.append(jnp.where(lanes >= subs + start, scaled, 0.0))
        inverse_rows.append(jnp.where(lanes < subs + start, scaled, jnp.where(lanes == subs + start, root, 0.0)))
    return jnp.concatenate(upper_rows, axis=0), jnp.concatenate(inverse_rows, axis=0)


def kernel(
    sizes,
    blocks_hbm, rows_ref, cols_ref, count_ref, sub_ref,
    out_ref, factor_ref,
    blk, panel, weights, table, ctable, sums, own1, send1, recv1, send2, recv2, ybuf, ygather,
    gram_own, gram_a, gram_b, gram_sb, gram_full,
    blk_sem, p_send, p_recv, s1_send, s1_recv, s2_send, s2_recv, y_send, y_recv,
    a_send, a_recv, b_send, b_recv, c_send, c_recv,
):
    n_row, n_col, n_pol, slots, bs, width = sizes
    half = width // 2
    group = n_col * n_pol
    chunk = half // group
    scale = 1.0 / (2.0 * bs * n_row * group)
    dense = n_row <= slots
    kmax = n_row if dense else slots
    r, c, p = lax.axis_index("row"), lax.axis_index("col"), lax.axis_index("pol")
    g = c * n_pol + p

    load = pltpu.make_async_copy(blocks_hbm, blk.at[pl.ds(0, slots)], blk_sem)
    load.start()

    def row_peer(d):
        return {"row": lax.rem(r + d, n_row)}

    def group_peer(e):
        j = lax.rem(g + e, group)
        return j, {"col": lax.div(j, n_pol), "pol": lax.rem(j, n_pol)}

    barrier = pltpu.get_barrier_semaphore()
    for d in range(1, n_row):
        pl.semaphore_signal(barrier, inc=1, device_id=row_peer(d), device_id_type=pl.DeviceIdType.MESH)
    for e in range(1, group):
        pl.semaphore_signal(barrier, inc=1, device_id=group_peer(e)[1], device_id_type=pl.DeviceIdType.MESH)
    pl.semaphore_wait(barrier, n_row - 1 + group - 1)

    def remote(src, dst, send, recv, device):
        return pltpu.make_async_remote_copy(
            src_ref=src, dst_ref=dst, send_sem=send, recv_sem=recv,
            device_id=device, device_id_type=pl.DeviceIdType.MESH,
        )

    gathers = [
        remote(sub_ref, panel.at[d], p_send.at[d], p_recv.at[d], row_peer(d))
        for d in range(1, n_row)
    ]
    for copy in gathers:
        copy.start()

    live = count_ref[0, 0, 0]
    for t in range(group):
        for k in range(kmax):
            if dense:
                slot = jnp.int32(slots)
                for s in range(slots):
                    match = (rows_ref[0, 0, 0, s] == t) & (cols_ref[0, 0, 0, s] == k) & (live > s)
                    slot = jnp.where(match, jnp.int32(s), slot)
            else:
                match = (rows_ref[0, 0, 0, k] == t) & (live > k)
                slot = jnp.where(match, jnp.int32(k), jnp.int32(slots))
            table[t * kmax + k] = slot
    if not dense:
        for k in range(kmax):
            ctable[k] = cols_ref[0, 0, 0, k]
    blk[slots] = jnp.zeros_like(blk[slots])

    def place(q, part):
        real, imag = part[:, :half], part[:, half:]
        weights[q, :bs] = part
        weights[q, bs:] = jnp.concatenate([-imag, real], axis=1)

    place(r, sub_ref[...])
    for d in range(1, n_row):
        gathers[d - 1].wait_recv()
        place(lax.rem(r - d + n_row, n_row), panel[d])
    load.wait()

    def product(t):
        if dense:
            left, right = [], []
            for k in range(kmax):
                slot = table[t * kmax + k]
                left += [blk[slot, 0], blk[slot, 1]]
                right.append(weights[k])
            return jnp.dot(
                jnp.concatenate(left, axis=1), jnp.concatenate(right, axis=0), preferred_element_type=F32
            )
        sums[...] = jnp.zeros_like(sums)

        def add(k, carry):
            slot, col = table[t * kmax + k], ctable[k]
            lhs = jnp.concatenate([blk[slot, 0], blk[slot, 1]], axis=1)
            sums[...] += jnp.dot(lhs, weights[col], preferred_element_type=F32)
            return carry

        lax.fori_loop(0, kmax, add, 0)
        return sums[...]

    def iteration(it, carry):
        firsts, seconds = [], []
        for d in list(range(1, n_col)) + [0]:
            cc = lax.rem(c + d, n_col)
            send1[it, d] = product(cc * n_pol + 1 - p)
            copy = remote(send1.at[it, d], recv1.at[it, d], s1_send.at[it, d], s1_recv.at[it, d], {"pol": 1 - p})
            copy.start()
            firsts.append(copy)
            own1[d] = product(cc * n_pol + p)
            if d:
                copy.wait_recv()
                send2[it, d] = own1[d] + recv1[it, d]
                copy = remote(
                    send2.at[it, d], recv2.at[it, d], s2_send.at[it, d], s2_recv.at[it, d], {"col": cc}
                )
                copy.start()
                seconds.append(copy)
        firsts[-1].wait_recv()
        image = own1[0] + recv1[it, 0]
        for d in range(1, n_col):
            seconds[d - 1].wait_recv()
            image = image + recv2[it, d]
        ybuf[it] = image

        tall = jnp.concatenate([image[:, :half], image[:, half:]], axis=0)
        gram_own[it] = lax.dot_general(
            tall, tall, (((0,), (0,)), ((), ())), precision=HI, preferred_element_type=F32
        )
        stage_a = []
        for e in range(1, group):
            j, device = group_peer(e)
            src = gram_own.at[it, pl.ds(pl.multiple_of(j * chunk, 8), chunk)]
            copy = remote(src, gram_a.at[it, e], a_send.at[it, e], a_recv.at[it, e], device)
            copy.start()
            stage_a.append(copy)
        mine = pl.ds(pl.multiple_of(g * chunk, 8), chunk)
        part = gram_own[it, mine]
        for e in range(1, group):
            stage_a[e - 1].wait_recv()
            part = part + gram_a[it, e]
        gram_sb[it] = part
        gram_b[it, r] = part
        stage_b = []
        for d in range(1, n_row):
            copy = remote(
                gram_sb.at[it], gram_b.at[it, r], b_send.at[it, d], b_recv.at[it, d], row_peer(d)
            )
            copy.start()
            stage_b.append(copy)

        def image_copy(d):
            return remote(ybuf.at[0], ygather.at[d], y_send.at[d], y_recv.at[d], row_peer(d))

        @pl.when(it < ITERS - 1)
        def _():
            for d in range(1, n_row):
                image_copy(d).start()

        for d in range(1, n_row):
            stage_b[d - 1].wait_recv()
        total = gram_b[it, 0]
        for q in range(1, n_row):
            total = total + gram_b[it, q]
        gram_full[it, mine] = total * scale
        stage_c = []
        for e in range(1, group):
            copy = remote(
                gram_full.at[it, mine], gram_full.at[it, mine], c_send.at[it, e], c_recv.at[it, e], group_peer(e)[1]
            )
            copy.start()
            stage_c.append(copy)
        for e in range(1, group):
            back = lax.rem(g - e + group, group)
            theirs = gram_full.at[it, pl.ds(pl.multiple_of(back * chunk, 8), chunk)]
            remote(theirs, theirs, c_send.at[it, e], c_recv.at[it, e], group_peer(e)[1]).wait_recv()

        upper, inverse = factor_and_inverse(gram_full[it])
        turned = inverse.T
        blank = jnp.zeros_like(turned)
        solve = jnp.concatenate(
            [jnp.concatenate([turned, blank], axis=1), jnp.concatenate([blank, turned], axis=1)], axis=0
        )

        def normal(rows):
            return jnp.dot(rows, solve, precision=HI, preferred_element_type=F32)

        @pl.when(it < ITERS - 1)
        def _():
            place(r, normal(ybuf[0]).astype(BF16))
            for d in range(1, n_row):
                image_copy(d).wait()
                place(lax.rem(r - d + n_row, n_row), normal(ygather[d]).astype(BF16))

        @pl.when(it == ITERS - 1)
        def _():
            out_ref[...] = normal(ybuf[ITERS - 1])
            factor_ref[...] = upper.T

        for copy in firsts + seconds + stage_a + stage_b + stage_c:
            copy.wait_send()
        return carry

    lax.fori_loop(0, ITERS, iteration, 0)
    for copy in gathers:
        copy.wait_send()


def on_device(tcc_blocks, slot_rows, slot_cols, slot_count, subspace):
    bs, width = subspace.shape
    half = width // 2
    n_row, n_col, n_pol = lax.axis_size("row"), lax.axis_size("col"), lax.axis_size("pol")
    group = n_col * n_pol
    slots = tcc_blocks.shape[3]
    chunk = half // group
    kmax = n_row if n_row <= slots else slots
    sizes = (n_row, n_col, n_pol, slots, bs, width)
    dma = pltpu.SemaphoreType.DMA
    vmem = pl.BlockSpec(memory_space=pltpu.VMEM)
    smem = pl.BlockSpec(memory_space=pltpu.SMEM)
    return pl.pallas_call(
        functools.partial(kernel, sizes),
        out_shape=(
            jax.ShapeDtypeStruct((bs, width), F32),
            jax.ShapeDtypeStruct((half, half), F32),
        ),
        in_specs=[pl.BlockSpec(memory_space=pl.ANY), smem, smem, smem, vmem],
        out_specs=(vmem, vmem),
        scratch_shapes=[
            pltpu.VMEM((slots + 1, 2, bs, bs), BF16),
            pltpu.VMEM((n_row, bs, width), BF16),
            pltpu.VMEM((n_row, 2 * bs, width), BF16),
            pltpu.SMEM((group * kmax,), jnp.int32),
            pltpu.SMEM((slots,), jnp.int32),
            pltpu.VMEM((bs, width), F32),
            pltpu.VMEM((n_col, bs, width), F32),
            pltpu.VMEM((ITERS, n_col, bs, width), F32),
            pltpu.VMEM((ITERS, n_col, bs, width), F32),
            pltpu.VMEM((ITERS, n_col, bs, width), F32),
            pltpu.VMEM((ITERS, n_col, bs, width), F32),
            pltpu.VMEM((ITERS, bs, width), F32),
            pltpu.VMEM((n_row, bs, width), F32),
            pltpu.VMEM((ITERS, half, half), F32),
            pltpu.VMEM((ITERS, group, chunk, half), F32),
            pltpu.VMEM((ITERS, n_row, chunk, half), F32),
            pltpu.VMEM((ITERS, chunk, half), F32),
            pltpu.VMEM((ITERS, half, half), F32),
            dma,
            dma((n_row,)), dma((n_row,)),
            dma((ITERS, n_col)), dma((ITERS, n_col)),
            dma((ITERS, n_col)), dma((ITERS, n_col)),
            dma((n_row,)), dma((n_row,)),
            dma((ITERS, group)), dma((ITERS, group)),
            dma((ITERS, n_row)), dma((ITERS, n_row)),
            dma((ITERS, group)), dma((ITERS, group)),
        ],
        compiler_params=pltpu.CompilerParams(
            collective_id=0, has_side_effects=True, vmem_limit_bytes=56 * 1024 * 1024
        ),
    )(tcc_blocks.reshape(slots, 2, bs, bs), slot_rows, slot_cols, slot_count, subspace)


def solution(mesh):
    placed = (
        P(("clip", "row"), "col", "pol", None, None, None, None),
        P(("clip", "row"), "col", "pol", None),
        P(("clip", "row"), "col", "pol", None),
        P(("clip", "row"), "col", "pol"),
        P(("clip", "row", "col", "pol"), None),
    )
    return jax.shard_map(
        on_device,
        mesh=mesh,
        in_specs=placed,
        out_specs=(P(("clip", "row", "col", "pol"), None), P("clip", None)),
        check_vma=False,
    )
```

time: 594 us -> 86.7 us (0.15)
  waiting for transfers between devices: 382 us -> 0 us
  Pallas kernels: 0 us -> 82.1 us
  loops' own time: 56.6 us -> 0 us
  other arithmetic: 50.6 us -> 0 us
  blocking collectives: 35 us -> 0 us
  local copies, waits for them, and re-layouts: 30.9 us -> 3.14 us
  matrix products: 20 us -> 0 us
  between operations: 13.9 us -> 1.29 us
    reduce_scatter x2 -> x0, waiting for transfers between devices: 211 us -> none  [on_device(): lax.psum_scatter(partial_value.reshape(col_group * block_size, full_width...]
    psum x2 -> x0, waiting for transfers between devices: 171 us -> none  [on_device(): gram_sum = lax.psum(local_gram, ('row', 'col', 'pol')) / (2.0 * order_total)]
    pallas_call x0 -> x1, Pallas kernels: none -> 82.1 us  [on_device(): pl.pallas_call(functools.partial(kernel, sizes), out_shape=(jax.ShapeDtyp...]
    another operation x2 -> x0, loops' own time: 56.6 us -> none  [accumulate(): return lax.fori_loop(jnp.int32(first), jnp.int32(last), visit_slot, running)]
    another operation x10 -> x0, other arithmetic: 46.3 us -> none  [the longest x6 24.8 us: on_device(): factor = jnp.linalg.cholesky(gram_sum)]
    all_gather x2 -> x0, blocking collectives: 35 us -> none  [on_device(): lax.all_gather(current, 'row', axis=0, tiled=True)]
    dynamic_slice x48 -> x0, local copies, waits for them, and re-layouts: 23.8 us -> none  [the longest x12 11 us: visit_slot(): target = row_ids[position]]
    dot_general x14 -> x0, matrix products: 19.2 us -> none  [the longest x12 14.7 us: visit_slot(): jnp.dot(block_data, fetch_rows(position), preferred_element_type=jnp.floa...]
  transfers between devices with their start and end apart: 4 -> 0, of which waited for: 4 -> 0; matrix products, arithmetic and copies ran while one was open for 0% -> 0% of each run, Pallas kernels for 0% -> 0%
where the time goes in v1:
time: 86.7 us; the launch traced here: 86.5 us
  Pallas kernels  82.1 us (95%)
  local copies, waits for them, and re-layouts  3.14 us (4%)
  between operations  1.29 us (1%)
    pallas_call x1, Pallas kernels, on_device(): pl.pallas_call(functools.partial(kernel, sizes), out_shape=(jax.ShapeDtyp...  82.1 us
    unnamed x2, local copies, waits for them, and re-layouts  3.14 us

profile of v1, /device:TPU:0, one launch (start us, length us, event | category | flops | bytes accessed | tf_op | source)
XLA Modules:
  0.0 86.5 jit_solution(1303070118592006374)
XLA Ops:
  1.3 82.1 %shard_map.68 = (f32[256,256]{1,0:T(8,128)}, f32[128,128]{1,0:T(8,128)}) custom-call(bf16[16,2,256,256]{3,2,1,0:T(8,128)(2,1)} %bitcast.1, s32[1,1,1,16]{3,2,1,0:T(1,128)} %rows_ref.1, s32[1,1,1,16]{3,2,1,0:T(1,128)} %cols_ref.1, s32[1,1,1]{2,1,0:T(1,128)S(6)} %copy.9.count_ref, bf16[256,256]{1,0:T(8,128)(2,1)} %sub_ref.1), custom_call_target="tpu_custom_call" | custom-call | tf_op jit(solution)/shard_map/pallas_call | solution.py:272
  83.4 1.7 %copy.10 = f32[256,256]{1,0:T(8,128)} copy(f32[256,256]{1,0:T(8,128)} %get-tuple-element.4) | data formatting | bytes 524288
  85.0 1.5 %copy.11 = f32[128,128]{1,0:T(8,128)} copy(f32[128,128]{1,0:T(8,128)} %get-tuple-element.5) | data formatting | bytes 131072

commit v2 on v1

--- a/solution.py
+++ b/solution.py
@@ -12,6 +12,7 @@
 BF16 = jnp.bfloat16
 HI = lax.Precision.HIGHEST
 PANEL = 8
+EARLY = 128
 
 
 def factor_and_inverse(gram):
@@ -56,15 +57,16 @@
     sizes,
     blocks_hbm, rows_ref, cols_ref, count_ref, sub_ref,
     out_ref, factor_ref,
-    blk, panel, weights, table, ctable, sums, own1, send1, recv1, send2, recv2, ybuf, ygather,
+    blk, panel, weights, table, ctable, sums, own1, send1, recv1, send2, recv2, ybuf, ygather, xbuf, late,
     gram_own, gram_a, gram_b, gram_sb, gram_full,
-    blk_sem, p_send, p_recv, s1_send, s1_recv, s2_send, s2_recv, y_send, y_recv,
+    blk_sem, p_send, p_recv, s1_send, s1_recv, s2_send, s2_recv, y_send, y_recv, x_send, x_recv,
     a_send, a_recv, b_send, b_recv, c_send, c_recv,
 ):
     n_row, n_col, n_pol, slots, bs, width = sizes
     half = width // 2
     group = n_col * n_pol
     chunk = half // group
+    early = EARLY
     scale = 1.0 / (2.0 * bs * n_row * group)
     dense = n_row <= slots
     kmax = n_row if dense else slots
@@ -94,12 +96,25 @@
             device_id=device, device_id_type=pl.DeviceIdType.MESH,
         )
 
-    gathers = [
-        remote(sub_ref, panel.at[d], p_send.at[d], p_recv.at[d], row_peer(d))
-        for d in range(1, n_row)
-    ]
-    for copy in gathers:
-        copy.start()
+    class Exchange:
+        def __init__(self, src, dst, send, recv):
+            self.copies = {
+                d: remote(src, dst.at[d], send.at[d], recv.at[d], row_peer(d)) for d in range(1, n_row)
+            }
+
+        def start(self):
+            for copy in self.copies.values():
+                copy.start()
+
+        def wait_recv(self, d):
+            self.copies[d].wait_recv()
+
+        def wait_send(self):
+            for copy in self.copies.values():
+                copy.wait_send()
+
+    first = Exchange(sub_ref, panel, p_send, p_recv)
+    first.start()
 
     live = count_ref[0, 0, 0]
     for t in range(group):
@@ -118,16 +133,19 @@
             ctable[k] = cols_ref[0, 0, 0, k]
     blk[slots] = jnp.zeros_like(blk[slots])
 
-    def place(q, part):
+    def place(q, part, low=0):
         real, imag = part[:, :half], part[:, half:]
-        weights[q, :bs] = part
-        weights[q, bs:] = jnp.concatenate([-imag, real], axis=1)
+        count = part.shape[0]
+        weights[q, low:low + count] = part
+        weights[q, bs + low:bs + low + count] = jnp.concatenate([-imag, real], axis=1)
 
     place(r, sub_ref[...])
     for d in range(1, n_row):
-        gathers[d - 1].wait_recv()
+        first.wait_recv(d)
         place(lax.rem(r - d + n_row, n_row), panel[d])
     load.wait()
+    image_part = Exchange(ybuf.at[0, pl.ds(0, early)], ygather, y_send, y_recv)
+    late_part = Exchange(xbuf.at[pl.ds(early, bs - early)], late, x_send, x_recv)
 
     def product(t):
         if dense:
@@ -190,30 +208,25 @@
         for e in range(1, group):
             stage_a[e - 1].wait_recv()
             part = part + gram_a[it, e]
+        stage_b = []
         gram_sb[it] = part
         gram_b[it, r] = part
-        stage_b = []
         for d in range(1, n_row):
             copy = remote(
                 gram_sb.at[it], gram_b.at[it, r], b_send.at[it, d], b_recv.at[it, d], row_peer(d)
             )
             copy.start()
             stage_b.append(copy)
-
-        def image_copy(d):
-            return remote(ybuf.at[0], ygather.at[d], y_send.at[d], y_recv.at[d], row_peer(d))
-
         @pl.when(it < ITERS - 1)
         def _():
-            for d in range(1, n_row):
-                image_copy(d).start()
-
-        for d in range(1, n_row):
-            stage_b[d - 1].wait_recv()
-        total = gram_b[it, 0]
+            image_part.start()
+
+        for copy in stage_b:
+            copy.wait_recv()
+        part = gram_b[it, 0]
         for q in range(1, n_row):
-            total = total + gram_b[it, q]
-        gram_full[it, mine] = total * scale
+            part = part + gram_b[it, q]
+        gram_full[it, mine] = part * scale
         stage_c = []
         for e in range(1, group):
             copy = remote(
@@ -238,10 +251,17 @@
 
         @pl.when(it < ITERS - 1)
         def _():
-            place(r, normal(ybuf[0]).astype(BF16))
+            xbuf[...] = normal(ybuf[0]).astype(BF16)
+            late_part.start()
+            place(r, xbuf[...])
             for d in range(1, n_row):
-                image_copy(d).wait()
+                image_part.wait_recv(d)
                 place(lax.rem(r - d + n_row, n_row), normal(ygather[d]).astype(BF16))
+            for d in range(1, n_row):
+                late_part.wait_recv(d)
+                place(lax.rem(r - d + n_row, n_row), late[d], early)
+            image_part.wait_send()
+            late_part.wait_send()
 
         @pl.when(it == ITERS - 1)
         def _():
@@ -253,8 +273,7 @@
         return carry
 
     lax.fori_loop(0, ITERS, iteration, 0)
-    for copy in gathers:
-        copy.wait_send()
+    first.wait_send()
 
 
 def on_device(tcc_blocks, slot_rows, slot_cols, slot_count, subspace):
@@ -290,7 +309,9 @@
             pltpu.VMEM((ITERS, n_col, bs, width), F32),
             pltpu.VMEM((ITERS, n_col, bs, width), F32),
             pltpu.VMEM((ITERS, bs, width), F32),
-            pltpu.VMEM((n_row, bs, width), F32),
+            pltpu.VMEM((n_row, EARLY, width), F32),
+            pltpu.VMEM((bs, width), BF16),
+            pltpu.VMEM((n_row, bs - EARLY, width), BF16),
             pltpu.VMEM((ITERS, half, half), F32),
             pltpu.VMEM((ITERS, group, chunk, half), F32),
             pltpu.VMEM((ITERS, n_row, chunk, half), F32),
@@ -300,6 +321,7 @@
             dma((n_row,)), dma((n_row,)),
             dma((ITERS, n_col)), dma((ITERS, n_col)),
             dma((ITERS, n_col)), dma((ITERS, n_col)),
+            dma((n_row,)), dma((n_row,)),
             dma((n_row,)), dma((n_row,)),
             dma((ITERS, group)), dma((ITERS, group)),
             dma((ITERS, n_row)), dma((ITERS, n_row)),

time: 86.7 us -> 80.1 us (0.924)
  Pallas kernels: 82.1 us -> 75.5 us
    pallas_call x1, Pallas kernels: 82.1 us -> 75.5 us  [on_device(): pl.pallas_call(functools.partial(kernel, sizes), out_shape=(jax.ShapeDtyp...]
where the time goes in v2:
time: 80.1 us; the launch traced here: 79.9 us
  Pallas kernels  75.5 us (94%)
  local copies, waits for them, and re-layouts  3.14 us (4%)
  between operations  1.29 us (2%)
    pallas_call x1, Pallas kernels, on_device(): pl.pallas_call(functools.partial(kernel, sizes), out_shape=(jax.ShapeDtyp...  75.5 us
    unnamed x2, local copies, waits for them, and re-layouts  3.14 us

profile of v2, /device:TPU:0, one launch (start us, length us, event | category | flops | bytes accessed | tf_op | source)
XLA Modules:
  0.0 79.9 jit_solution(14473744603498609354)
XLA Ops:
  1.3 75.5 %shard_map.68 = (f32[256,256]{1,0:T(8,128)}, f32[128,128]{1,0:T(8,128)}) custom-call(bf16[16,2,256,256]{3,2,1,0:T(8,128)(2,1)} %bitcast.1, s32[1,1,1,16]{3,2,1,0:T(1,128)} %rows_ref.1, s32[1,1,1,16]{3,2,1,0:T(1,128)} %cols_ref.1, s32[1,1,1]{2,1,0:T(1,128)S(6)} %copy.9.count_ref, bf16[256,256]{1,0:T(8,128)(2,1)} %sub_ref.1), custom_call_target="tpu_custom_call" | custom-call | tf_op jit(solution)/shard_map/pallas_call | solution.py:291
  76.8 1.7 %copy.10 = f32[256,256]{1,0:T(8,128)} copy(f32[256,256]{1,0:T(8,128)} %get-tuple-element.4) | data formatting | bytes 524288
  78.4 1.5 %copy.11 = f32[128,128]{1,0:T(8,128)} copy(f32[128,128]{1,0:T(8,128)} %get-tuple-element.5) | data formatting | bytes 131072

commit v3 on v2

--- a/solution.py
+++ b/solution.py
@@ -12,7 +12,7 @@
 BF16 = jnp.bfloat16
 HI = lax.Precision.HIGHEST
 PANEL = 8
-EARLY = 128
+EARLY = 96
 
 
 def factor_and_inverse(gram):
@@ -251,8 +251,9 @@
 
         @pl.when(it < ITERS - 1)
         def _():
-            xbuf[...] = normal(ybuf[0]).astype(BF16)
+            xbuf[early:] = normal(ybuf[0, early:]).astype(BF16)
             late_part.start()
+            xbuf[:early] = normal(ybuf[0, :early]).astype(BF16)
             place(r, xbuf[...])
             for d in range(1, n_row):
                 image_part.wait_recv(d)

time: 80.1 us -> 79.6 us (level)
  no operation moved by 1% of the time
where the time goes in v3:
time: 79.6 us; the launch traced here: 79.3 us
  Pallas kernels  74.9 us (94%)
  local copies, waits for them, and re-layouts  3.14 us (4%)
  between operations  1.29 us (2%)
    pallas_call x1, Pallas kernels, on_device(): pl.pallas_call(functools.partial(kernel, sizes), out_shape=(jax.ShapeDtyp...  74.9 us
    unnamed x2, local copies, waits for them, and re-layouts  3.14 us

profile of v3, /device:TPU:0, one launch (start us, length us, event | category | flops | bytes accessed | tf_op | source)
XLA Modules:
  0.0 79.3 jit_solution(15035772543176650278)
XLA Ops:
  1.3 74.9 %shard_map.68 = (f32[256,256]{1,0:T(8,128)}, f32[128,128]{1,0:T(8,128)}) custom-call(bf16[16,2,256,256]{3,2,1,0:T(8,128)(2,1)} %bitcast.1, s32[1,1,1,16]{3,2,1,0:T(1,128)} %rows_ref.1, s32[1,1,1,16]{3,2,1,0:T(1,128)} %cols_ref.1, s32[1,1,1]{2,1,0:T(1,128)S(6)} %copy.9.count_ref, bf16[256,256]{1,0:T(8,128)(2,1)} %sub_ref.1), custom_call_target="tpu_custom_call" | custom-call | tf_op jit(solution)/shard_map/pallas_call | solution.py:292
  76.2 1.7 %copy.10 = f32[256,256]{1,0:T(8,128)} copy(f32[256,256]{1,0:T(8,128)} %get-tuple-element.4) | data formatting | bytes 524288
  77.9 1.5 %copy.11 = f32[128,128]{1,0:T(8,128)} copy(f32[128,128]{1,0:T(8,128)} %get-tuple-element.5) | data formatting | bytes 131072
